TPU v7x, 512 devices: a whole 4x8x8 slice. The times are simulated.
512 devices in a mesh: seq: 16 (over y, z_lo), res: 32 (over x, z_hi, core).
Axes of the slice: x: 4, y: 8, z: 8 (z_hi: 4, z_lo: 2; z = z_hi * 2 + z_lo), core: 2. Of those that a mesh axis runs over, the one named last changes fastest.
Arguments:
- alignment_embedding: bfloat16 [256, 1024, 256], P('seq', 'res'), may hold values from -6 to 6
- heed_layer_gain: float32 [256], replicated, may hold values from 0.25 to 1.75
- heed_layer_shift: float32 [256], replicated, may hold values from -1.75 to 1.75
- probe_weights: bfloat16 [256, 256], replicated, may hold values from -48 to 48
- lookup_weights: bfloat16 [256, 256], replicated, may hold values from -1 to 1
- content_weights: bfloat16 [256, 256], replicated, may hold values from -0.375 to 0.375
- sigmoid_weights: bfloat16 [256, 256], replicated, may hold values from -0.375 to 0.375
- sigmoid_shift: float32 [256], replicated, may hold values from -6 to 6
- final_weights: bfloat16 [256, 256], replicated, may hold values from -1.5 to 1.5
- final_shift: float32 [256], replicated, may hold values from -1.75 to 1.75
- tensor_layer_gain: float32 [256], replicated, may hold values from 0.25 to 1.75
- tensor_layer_shift: float32 [256], replicated, may hold values from -1.75 to 1.75
- first_factor_weights: bfloat16 [256, 32], replicated, may hold values from -0.375 to 0.375
- second_factor_weights: bfloat16 [256, 32], replicated, may hold values from -0.375 to 0.375
- couple_weights: bfloat16 [1024, 128], replicated, may hold values from -3 to 3
- couple_shift: float32 [128], replicated, may hold values from -1.75 to 1.75
Outputs:
- updated: bfloat16 [256, 1024, 256], P('seq', 'res')
- pair_update: bfloat16 [1024, 1024, 128], P('seq', 'res')
All inputs are finite; a program needn't handle non-finite values.
Results may differ from a plain program's by a relative error of at most 0.02.
Values may be sent and summed in bfloat16 or wider, within the bound.
A program may use at most 128 MiB of HBM per device.

v0:
```python
import jax
import jax.numpy as jnp
from jax import lax
from jax.sharding import PartitionSpec as P

HEAD_TOTAL = 8
HEAD_WIDTH = 32
FACTOR_FEATURES = 32


def from_root(value, axis, source):
    kept = jnp.where(lax.axis_index(axis) == source, value, 0).astype(value.dtype)
    return lax.psum(kept, axis)


def layer_norm(values, scale, offset):
    center = values - jnp.mean(values, axis=-1, keepdims=True)
    spread = jnp.mean(center * center, axis=-1, keepdims=True)
    return center * lax.rsqrt(spread + 1e-05) * scale + offset


def attend(
    normed_q,
    keys,
    values,
    probe_weights,
    sigmoid_weights,
    sigmoid_shift,
    final_weights,
    final_shift,
):
    query_rows, width_rows, channels = normed_q.shape
    key_rows = keys.shape[0]
    queries = jnp.dot(normed_q, probe_weights, preferred_element_type=jnp.float32).astype(
        jnp.bfloat16
    )
    queries = queries.reshape(query_rows, width_rows, HEAD_TOTAL, HEAD_WIDTH)
    keys = keys.reshape(key_rows, width_rows, HEAD_TOTAL, HEAD_WIDTH)
    values = values.reshape(key_rows, width_rows, HEAD_TOTAL, HEAD_WIDTH)
    scores = jnp.einsum(
        "srhd,trhd->rhst", queries, keys, preferred_element_type=jnp.float32
    ) / jnp.sqrt(jnp.float32(HEAD_WIDTH))
    weights = jax.nn.softmax(scores, axis=-1).astype(jnp.bfloat16)
    mixed = jnp.einsum("rhst,trhd->srhd", weights, values, preferred_element_type=jnp.float32)
    mixed = mixed.reshape(query_rows, width_rows, HEAD_TOTAL * HEAD_WIDTH)
    gate = jax.nn.sigmoid(
        jnp.dot(normed_q, sigmoid_weights, preferred_element_type=jnp.float32) + sigmoid_shift
    )
    gated = (mixed * gate).astype(jnp.bfloat16)
    return (jnp.dot(gated, final_weights, preferred_element_type=jnp.float32) + final_shift).astype(
        jnp.bfloat16
    )


def local(
    alignment_embedding,
    heed_layer_gain,
    heed_layer_shift,
    probe_weights,
    lookup_weights,
    content_weights,
    sigmoid_weights,
    sigmoid_shift,
    final_weights,
    final_shift,
    tensor_layer_gain,
    tensor_layer_shift,
    first_factor_weights,
    second_factor_weights,
    couple_weights,
    couple_shift,
):
    seq_count = lax.axis_size("seq")
    res_count = lax.axis_size("res")
    given_tensor = alignment_embedding.astype(jnp.float32)
    standardized = layer_norm(given_tensor, heed_layer_gain, heed_layer_shift).astype(jnp.bfloat16)
    local_seqs, local_res, channels = standardized.shape
    per_owner = local_res // seq_count
    grouped = standardized.reshape(local_seqs, seq_count, per_owner, channels)
    block = lax.all_to_all(grouped, "seq", split_axis=1, concat_axis=0, tiled=True)
    block_rows = block.shape[0]
    block_res = block.shape[2]
    flat_block = block.reshape(block_rows, block_res, channels)
    keys = jnp.dot(flat_block, lookup_weights, preferred_element_type=jnp.float32).astype(
        jnp.bfloat16
    )
    values = jnp.dot(flat_block, content_weights, preferred_element_type=jnp.float32).astype(
        jnp.bfloat16
    )
    keys, values = (keys, values)
    result = attend(
        flat_block,
        keys,
        values,
        probe_weights,
        sigmoid_weights,
        sigmoid_shift,
        final_weights,
        final_shift,
    )
    turned = result.reshape(block_rows, 1, block_res, channels)
    returned = lax.all_to_all(turned, "seq", split_axis=0, concat_axis=1, tiled=True)
    weighted_mixture = returned.reshape(local_seqs, local_res, channels)
    updated = (given_tensor + weighted_mixture.astype(jnp.float32)).astype(jnp.bfloat16)
    outer_normed = layer_norm(
        updated.astype(jnp.float32), tensor_layer_gain, tensor_layer_shift
    ).astype(jnp.bfloat16)
    left = jnp.dot(outer_normed, first_factor_weights, preferred_element_type=jnp.float32).astype(
        jnp.bfloat16
    )
    right = jnp.dot(outer_normed, second_factor_weights, preferred_element_type=jnp.float32).astype(
        jnp.bfloat16
    )
    shard_span = res_count // seq_count
    row_index = lax.axis_index("seq")
    left_all, right_all = (
        lax.all_gather(left, "seq", axis=0, tiled=True),
        lax.all_gather(right, "seq", axis=0, tiled=True),
    )
    row_left = jnp.concatenate(
        [
            from_root(left_all, "res", row_index * shard_span + offset)
            for offset in range(shard_span)
        ],
        axis=1,
    )
    total_seqs = right_all.shape[0]
    row_count = row_left.shape[1]
    col_count = right_all.shape[1]
    outer = lax.dot_general(
        row_left.reshape(total_seqs, row_count * FACTOR_FEATURES),
        right_all.reshape(total_seqs, col_count * FACTOR_FEATURES),
        (((0,), (0,)), ((), ())),
        preferred_element_type=jnp.float32,
    )
    outer = (outer / total_seqs).astype(jnp.bfloat16)
    outer = (
        outer.reshape(row_count, FACTOR_FEATURES, col_count, FACTOR_FEATURES)
        .transpose(0, 2, 1, 3)
        .reshape(row_count, col_count, FACTOR_FEATURES * FACTOR_FEATURES)
    )
    pair_update = (
        jnp.dot(outer, couple_weights, preferred_element_type=jnp.float32) + couple_shift
    ).astype(jnp.bfloat16)
    return (updated, pair_update)


def solution(mesh):
    placed = (
        P("seq", "res", None),
        P(),
        P(),
        P(),
        P(),
        P(),
        P(),
        P(),
        P(),
        P(),
        P(),
        P(),
        P(),
        P(),
        P(),
        P(),
    )
    return jax.shard_map(
        local,
        mesh=mesh,
        in_specs=placed,
        out_specs=(P("seq", "res", None), P("seq", "res", None)),
        check_vma=False,
    )
```

profile of v0, /device:TPU:1, one launch (start us, length us, event | category | flops | bytes accessed | tf_op | source)
XLA Modules:
  0.0 498.4 jit_solution(11152403138252088973)
XLA Ops:
  7.2 0.0 copy-start
  7.2 1.1 convert_reduce_fusion
  8.3 1.2 fusion.19
  9.6 1.2 fusion.22
  10.7 0.2 copy.37
  10.9 19.9 %all_to_all.24 = bf16[16,16,2,256]{3,0,2,1:T(8,128)(2,1)S(1)} all-to-all(bf16[16,16,2,256]{3,0,2,1:T(8,128)(2,1)S(1)} %bitcast.68), channel_id=1, replica_groups=mesh['seq'=16,'res'=32] {'seq'}, dimensions={1} | all-to-all | bytes 524288 | tf_op jit(solution)/shard_map/all_to_all | solution.py:80
  30.8 1.2 convolution_convert_fusion
  32.0 1.2 convolution_convert_fusion.1
  33.1 1.2 convolution_convert_fusion.2
  34.3 3.5 fusion.46
  37.8 0.0 copy-start.4
  37.8 0.0 copy-start.5
  37.8 0.0 copy-start.8
  37.8 0.0 copy-start.9
  37.8 2.7 fusion.5
  40.5 0.0 copy-start.1
  40.5 0.2 copy.43
  40.7 0.0 copy-done.4
  40.7 0.0 copy-done.5
  40.7 0.0 copy-done.8
  40.8 0.0 copy-done.9
  40.8 0.0 copy-start.6
  40.8 0.0 copy-start.10
  40.8 0.0 copy-start.11
  40.8 0.4 fusion.14
  41.2 1.0 copy.44
  42.2 3.5 all-to-all-start.1
  45.7 0.0 all-reduce.3.cloned.1.call-start
  45.8 9.5 %all-to-all-done.1 = bf16[256,1,2,256]{3,2,1,0:T(2,128)(2,1)S(1)} async-done(((bf16[256,1,2,256]{3,2,1,0:T(2,128)(2,1)}), bf16[256,1,2,256]{3,2,1,0:T(2,128)(2,1)S(1)}, u32[]{:S(2)}, u32[]{:S(2)}) %all-to-all-start.1) | async-done | bytes 262176 | tf_op jit(solution)/shard_map/all_to_all | solution.py:102
  55.3 0.2 convert_bitcast_fusion
  55.5 0.3 copy.45
  55.8 0.4 reshape.88
  56.2 0.0 copy-done.1
  56.2 0.1 convert_reduce_fusion.1
  56.3 0.0 copy-start.2
  56.4 0.3 fusion.23
  56.6 0.0 copy-done.6
  56.6 0.0 copy-done.10
  56.7 0.0 copy-done.11
  56.7 0.3 convolution_convert_fusion.4
  57.0 48.1 %all_gather.6 = bf16[256,32,32]{2,1,0:T(8,128)(2,1)S(1)} all-gather(bf16[16,32,32]{2,1,0:T(8,128)(2,1)S(1)} %convolution_convert_fusion.4), channel_id=1, replica_groups=mesh['seq'=16,'res'=32] {'seq'}, dimensions={0}, use_global_device_ids=true | all-gather | bytes 557056 | tf_op jit(solution)/shard_map/all_gather | solution.py:117
  105.1 0.0 copy-start.7
  105.1 2.2 broadcast_select_fusion.1
  107.3 0.0 all-reduce.3.cloned.1.call-update
  107.3 0.0 copy-done.2
  107.4 0.0 copy-done.7
  107.4 0.3 convolution_convert_fusion.3
  107.7 63.3 %all_gather.7 = bf16[256,32,32]{2,1,0:T(8,128)(2,1)S(1)} all-gather(bf16[16,32,32]{2,1,0:T(8,128)(2,1)S(1)} %convolution_convert_fusion.3), channel_id=1, replica_groups=mesh['seq'=16,'res'=32] {'seq'}, dimensions={0}, use_global_device_ids=true | all-gather | bytes 557056 | tf_op jit(solution)/shard_map/all_gather | solution.py:118
  171.0 1.7 copy.48
  172.6 261.2 %all-reduce.3.cloned.1.call-done = (bf16[256,32,32]{2,1,0:T(8,128)(2,1)}, bf16[256,32,32]{2,1,0:T(8,128)(2,1)}) async-done(((bf16[256,32,32]{2,1,0:T(8,128)(2,1)}, bf16[256,32,32]{2,1,0:T(8,128)(2,1)}), (bf16[256,32,32]{2,1,0:T(8,128)(2,1)}, bf16[256,32,32]{2,1,0:T(8,128)(2,1)})) %all-reduce.3.cloned.1.call-update) | async-done | bytes 1048592 | tf_op jit(solution)/shard_map/psum | solution.py:13
  433.9 2.8 copy.47
  436.6 2.8 copy.46
  439.4 0.1 pad_maximum_fusion
  439.5 3.2 multiply_convert_fusion
  442.7 20.3 %reshape.86 = bf16[64,32,32,32]{3,2,1,0:T(8,128)(2,1)} reshape(bf16[2048,1024]{1,0:T(8,128)(2,1)} %multiply_convert_fusion) | data formatting | bytes 8388608 | tf_op jit(solution)/shard_map/reshape | solution.py:138
  463.0 0.0 copy-start.3
  463.0 21.6 %copy.49 = bf16[64,32,32,32]{0,3,2,1:T(8,128)(2,1)} copy(bf16[64,32,32,32]{3,1,2,0:T(8,128)(2,1)} %bitcast.60) | data formatting | bytes 8388608 | tf_op jit(solution)/shard_map/transpose | solution.py:139
  484.7 0.0 copy-done
  484.7 0.0 copy-done.3
  484.7 5.8 %fusion.6 = bf16[64,32,128]{2,0,1:T(8,128)(2,1)S(1)} fusion(bf16[64,32,1024]{0,2,1:T(8,128)(2,1)} %bitcast.61, f32[128]{0:T(128)S(1)} %copy-done.3, bf16[1024,128]{1,0:T(8,128)(2,1)S(1)} %copy-done), kind=kOutput, calls=%fused_computation.11 | convolution fusion | flops 537395200 | bytes 4981248 | tf_op jit(solution)/shard_map/dot_general | solution.py:143
  490.4 1.1 copy.51
  (5 shorter events, 0.0 us)
Async XLA Ops:
  7.2 477.5 %copy-start = (bf16[1024,128]{1,0:T(8,128)(2,1)S(1)}, bf16[1024,128]{1,0:T(8,128)(2,1)}, u32[]{:S(2)}) copy-start(bf16[1024,128]{1,0:T(8,128)(2,1)} %param.30) | copy-start | bytes 786436
  37.8 2.9 copy-start.4
  37.8 3.0 copy-start.5
  37.8 3.0 copy-start.8
  37.8 3.0 copy-start.9
  40.5 15.7 %copy-start.1 = (bf16[16,32,256]{2,1,0:T(8,128)(2,1)S(1)}, bf16[16,32,256]{2,1,0:T(8,128)(2,1)}, u32[]{:S(2)}) copy-start(bf16[16,32,256]{2,1,0:T(8,128)(2,1)} %param.16) | copy-start | bytes 786436
  40.8 15.9 %copy-start.6 = (bf16[256,32]{0,1:T(8,128)(2,1)S(1)}, bf16[256,32]{0,1:T(8,128)(2,1)}, u32[]{:S(2)}) copy-start(bf16[256,32]{0,1:T(8,128)(2,1)} %param.28) | copy-start | bytes 49156
  40.8 15.9 %copy-start.10 = (f32[256]{0:T(256)S(1)}, f32[256]{0:T(256)}, u32[]{:S(2)}) copy-start(f32[256]{0:T(256)} %param.27) | copy-start | bytes 3076
  40.8 15.9 %copy-start.11 = (f32[256]{0:T(256)S(1)}, f32[256]{0:T(256)}, u32[]{:S(2)}) copy-start(f32[256]{0:T(256)} %param.26) | copy-start | bytes 3076
  42.2 13.1 %all-to-all-start.1 = ((bf16[256,1,2,256]{3,2,1,0:T(2,128)(2,1)}), bf16[256,1,2,256]{3,2,1,0:T(2,128)(2,1)S(1)}, u32[]{:S(2)}, u32[]{:S(2)}) async-start(bf16[256,1,2,256]{3,2,1,0:T(2,128)(2,1)} %copy.44), calls=%async_computation.1 | async-start | bytes 524288 | tf_op jit(solution)/shard_map/all_to_all | solution.py:102
  45.7 388.1 %all-reduce.3.cloned.1.call-start = ((), (), s32[]{:S(2)}) async-start(), calls=%async_computation.2 | async-start | bytes 8388608 | tf_op jit(solution)/shard_map/psum | solution.py:13
  56.3 51.0 %copy-start.2 = (bf16[16,32,256]{2,1,0:T(8,128)(2,1)}, bf16[16,32,256]{2,1,0:T(8,128)(2,1)S(1)}, u32[]{:S(2)}) copy-start(bf16[16,32,256]{2,1,0:T(8,128)(2,1)S(1)} %get-tuple-element.7) | copy-start | bytes 786436
  105.1 2.3 copy-start.7
  463.0 21.6 %copy-start.3 = (f32[128]{0:T(128)S(1)}, f32[128]{0:T(128)}, u32[]{:S(2)}) copy-start(f32[128]{0:T(128)} %param.31) | copy-start | bytes 1540
Sparse Core Ops, SparseCore 0:
  107.5 326.3 all-reduce.2
where the time goes:
time: 500 us; the launch traced here: 498 us
  waiting for transfers between devices  271 us (54%)
  blocking collectives  131 us (26%)
  local copies, waits for them, and re-layouts  52.3 us (10%)
  matrix products  19.7 us (4%)
  between operations  14.4 us (3%)
  other arithmetic  6.47 us (1%)
    psum x1, waiting for transfers between devices, from_root(): return lax.psum(kept, axis)  261 us
    all_gather x1, blocking collectives, local(): lax.all_gather(right, 'seq', axis=0, tiled=True)  63.3 us
    all_gather x1, blocking collectives, local(): lax.all_gather(left, 'seq', axis=0, tiled=True)  48.1 us
    transpose x1, local copies, waits for them, and re-layouts, local(): outer = outer.reshape(row_count, FACTOR_FEATURES, col_count, FACTOR_FEATU...  21.6 us
    reshape x1, local copies, waits for them, and re-layouts, local(): outer.reshape(row_count, FACTOR_FEATURES, col_count, FACTOR_FEATURES)  20.3 us
    all_to_all x1, blocking collectives, local(): lax.all_to_all(grouped, 'seq', split_axis=1, concat_axis=0, tiled=True)  19.9 us
  transfers between devices with their start and end apart: 2, of which 2 were waited for; matrix products, arithmetic and copies ran while one was open for 0% of the time, Pallas kernels for 0%

commit v1 on v0

v1 whole, which is shorter than its diff:
```python
import functools

import jax
import jax.numpy as jnp
from jax import lax
from jax.experimental import pallas as pl
from jax.experimental.pallas import tpu as pltpu
from jax.sharding import PartitionSpec as P

HEADS = 8
WIDTH = 32
BF16 = jnp.bfloat16
F32 = jnp.float32
MESH = pl.DeviceIdType.MESH
SPREAD = (4, 5, 3, 6, 2, 7, 1)


def norm_rows(values, scale, offset):
    center = values - jnp.mean(values, axis=-1, keepdims=True)
    spread = jnp.mean(center * center, axis=-1, keepdims=True)
    return center * lax.rsqrt(spread + 1e-05) * scale + offset


def dot(a, b):
    return jnp.dot(a, b, preferred_element_type=F32)


def dot_t(a, b):
    return lax.dot_general(a, b, (((1,), (1,)), ((), ())), preferred_element_type=F32)


def relay_of(p, y, zl):
    x, zh = p // 4, p % 4
    y_to, zl_to = p // 2, p % 2
    k = (y - y_to + 12) % 8
    dx = (2 * (k // 4) + 3 * (k % 2)) % 4
    far = ((k + 2) // 4) % 2
    e = (zl + zl_to) % 2
    s = 2 * zl_to - 1
    dz = (1 - e) * far * s + e * (far * 2 - (1 - far) * s)
    return (x + dx) % 4, (zh + dz + 8) % 4


def chunk_at(p, x, zh):
    x0, zh0 = p // 4, p % 4
    zl_to = p % 2
    s = 2 * zl_to - 1
    w = (x0 - x + 4) % 4
    u = ((zh - zh0 + 4) * (s + 4)) % 4
    e = u // 2
    far = ((u + 1) // 2) % 2
    k = w + (1 - far) * 4 * (w // 2) + 2 * far
    return (p // 2 + k + 4) % 8, (e + zl_to) % 2


def kernel(
    x_hbm, gain1, shift1, wq_hbm, wk_hbm, wv_hbm, wg_hbm, bg, wf_hbm, bf, gain2, shift2,
    w1_hbm, w2_hbm, wc_hbm, bc,
    upd_out, pair_out,
    xv, x32, xt, xg, wq, wk, wv, wg, wf, w1, w2, wc, w32, wt, w12t, vtx, gated_t, bd,
    upd, upd_all, lt, rt, left, right, r32, right_p, outer, pair,
    load_sem, a_send, a_recv, u_send, u_recv, p_send, p_recv, ry_send, ry_recv, rz_send, rz_recv,
    lz_send, lz_recv, lx_send, lx_recv, lc_send, lc_recv,
):
    q = lax.axis_index("seq")
    r = lax.axis_index("res")
    y, zl = q // 2, q % 2
    x, zh, c = r // 8, (r // 2) % 4, r % 2
    plane = r // 2

    def res(x_, zh_, c_):
        return (x_ * 4 + zh_) * 2 + c_

    def send(src, dst, ss, rs, dev):
        copy = pltpu.make_async_remote_copy(
            src_ref=src, dst_ref=dst, send_sem=ss, recv_sem=rs, device_id=dev, device_id_type=MESH
        )
        return copy

    seq_dev = [((q + k) % 16, r) for k in range(16)]
    y_dev = [(((y + k) % 8) * 2 + zl, r) for k in range(8)]
    zl_dev = (y * 2 + 1 - zl, r)
    zh_dev = [(q, res(x, (zh + k) % 4, c)) for k in range(4)]
    x_dev = [(q, res((x + k) % 4, zh, c)) for k in range(4)]
    core_dev = (q, res(x, zh, 1 - c))
    relay_x, relay_zh = relay_of(plane, y, zl)
    relay_dev = (plane, res(relay_x, relay_zh, c))
    from_y, from_zl = chunk_at(q, x, zh)
    from_dev = (from_y * 2 + from_zl, 2 * q + c)

    barrier = pltpu.get_barrier_semaphore()
    greet = seq_dev[1:] + zh_dev[1:] + x_dev[1:] + [core_dev, from_dev]
    for dev in greet:
        pl.semaphore_signal(barrier, inc=1, device_id=dev, device_id_type=MESH)

    loads = [
        pltpu.make_async_copy(a, b, load_sem.at[i])
        for i, (a, b) in enumerate(
            [(x_hbm, xv), (wc_hbm, wc), (wq_hbm, wq), (wk_hbm, wk), (wv_hbm, wv), (wg_hbm, wg),
             (wf_hbm, wf), (w1_hbm, w1), (w2_hbm, w2)]
        )
    ]
    for copy in loads:
        copy.start()

    loads[0].wait()

    @pl.loop(0, 16)
    def _(i):
        for half in range(2):
            x32[half, pl.ds(pl.multiple_of(i * 32, 32), 32), :] = xv[i, :, half * 128:(half + 1) * 128].astype(F32)

    @pl.loop(0, 32)
    def _(i):
        for half in range(2):
            xt[i, :, half * 128:(half + 1) * 128] = x32[half, pl.ds(i, 16, stride=32), :].astype(BF16)

    mine = pl.ds(pl.multiple_of(q * 16, 16), 16)
    for m in range(2):
        xg[m, mine, :] = xt[2 * q + m]

    pl.semaphore_wait(barrier, len(greet))
    order = (8, 7, 9, 6, 10, 5, 11, 4, 12, 3, 13, 2, 14, 1, 15)
    turn = {}
    for k in order:
        to = seq_dev[k][0]
        turn[k] = send(xt.at[pl.ds(2 * to, 2)], xg.at[:, mine, :], a_send.at[k], a_recv.at[k], seq_dev[k])
        turn[k].start()

    for copy in loads[1:]:
        copy.wait()
    wt[0:256, :] = wq[...].astype(F32).T.astype(BF16)
    wt[256:512, :] = wv[...].astype(F32).T.astype(BF16)
    wt[512:768, :] = wg[...].astype(F32).T.astype(BF16)
    w12t[0:32, :] = w1[...].astype(F32).T.astype(BF16)
    w12t[32:64, :] = w2[...].astype(F32).T.astype(BF16)
    vtx[:, 32:48, :] = jnp.ones((HEADS, 16, 256), BF16)
    w32[...] = wc[...].astype(F32)

    @pl.loop(0, 32)
    def _(b):
        block = w32[pl.ds(b, 32, stride=32), :].astype(BF16)
        zero = jnp.zeros((32, 128), BF16)
        for i in range(4):
            rows = pl.ds(pl.multiple_of(b * 128 + i * 32, 32), 32)
            for j in range(4):
                bd[rows, j * 128:(j + 1) * 128] = block if i == j else zero

    for k in order[::-1]:
        turn[k].wait_recv()

    for m in range(2):
        given = xg[m].astype(F32)
        normed = norm_rows(given, gain1[...], shift1[...]).astype(BF16)
        keys = dot(normed, wk[...]).astype(BF16)
        qvg = dot_t(wt[...], normed)
        queries_t = qvg[0:256].astype(BF16)
        vtx[:, 0:32, :] = qvg[256:512].astype(BF16).reshape(HEADS, WIDTH, 256)
        gate_t = 1.0 / (1.0 + jnp.exp(-(qvg[512:768] + bg[...])))
        for h in range(HEADS):
            span = slice(h * WIDTH, (h + 1) * WIDTH)
            scores = dot(keys[:, span], queries_t[span, :])
            top = jnp.max(scores, axis=0, keepdims=True)
            weights = jnp.exp((scores - top) * (1.0 / 32.0 ** 0.5)).astype(BF16)
            mixed = dot(vtx[h], weights)
            gated_t[span, :] = mixed[0:32] * (1.0 / mixed[32:33]) * gate_t[span, :]
        gated = gated_t[...].T.astype(BF16)
        attended = (dot(gated, wf[...]) + bf[...]).astype(BF16)
        updated = (given + attended.astype(F32)).astype(BF16)
        upd[m] = updated
        outer_normed = norm_rows(updated.astype(F32), gain2[...], shift2[...]).astype(BF16)
        both = dot_t(w12t[...], outer_normed).astype(BF16)
        lt[m * 32:(m + 1) * 32, :] = both[0:32]
        rt[m * 32:(m + 1) * 32, :] = both[32:64]

    def left_chunk(c_, y_, zl_):
        return left.at[c_ * 8 + y_, pl.ds(pl.multiple_of(zl_ * 64, 64), 64)]

    sent = []

    def go(*args):
        copy = send(*args)
        copy.start()
        sent.append(copy)
        return copy

    relay = go(lt, left_chunk(c, y, zl), p_send.at[0], p_recv.at[0], relay_dev)
    across = [go(rt, right.at[q], rz_send.at[0], rz_recv.at[0], zl_dev)]
    along = [None] * 8
    for k in SPREAD[::-1]:
        along[k] = go(rt, right.at[q], ry_send.at[k], ry_recv.at[k], y_dev[k])
    right[q] = rt[...]
    back = []
    for k in order:
        to = seq_dev[k][0]
        back.append(
            go(upd.at[:, pl.ds(pl.multiple_of(to * 16, 16), 16), :], upd_all.at[pl.ds(2 * q, 2)],
               u_send.at[k], u_recv.at[k], seq_dev[k])
        )
    for m in range(2):
        upd_all[2 * q + m] = upd[m, mine, :]

    def pass_on(cy, czl, i):
        here = left_chunk(c, cy, czl)
        xs = [go(here, here, lx_send.at[i * 3 + k - 1], lx_recv.at[i * 3 + k - 1], x_dev[k]) for k in (2, 1, 3)]
        go(here, here, lc_send.at[i], lc_recv.at[i], core_dev)
        return xs

    relay.wait_recv()
    here = left_chunk(c, from_y, from_zl)
    zs = {k: go(here, here, lz_send.at[k - 1], lz_recv.at[k - 1], zh_dev[k]) for k in (2, 1, 3)}
    pass_on(from_y, from_zl, 0)
    for k in SPREAD[::-1]:
        along[k].wait_recv()
        slot = ((y + 8 - k) % 8) * 2 + zl
        across.append(go(right.at[slot], right.at[slot], rz_send.at[k], rz_recv.at[k], zl_dev))
    for k in (1, 3, 2):
        zs[k].wait_recv()
        cy, czl = chunk_at(q, x, (zh + 4 - k) % 4)
        pass_on(cy, czl, k)
    for copy in across:
        copy.wait_recv()

    @pl.loop(0, 16)
    def _(i):
        for half in range(2):
            r32[half, pl.ds(pl.multiple_of(i * 64, 64), 64), :] = right[i, :, half * 128:(half + 1) * 128].astype(F32)

    @pl.loop(0, 32)
    def _(b):
        rows = pl.ds(pl.multiple_of(b * 32, 32), 32)
        for half in range(2):
            right_p[rows, half * 128:(half + 1) * 128] = r32[half, pl.ds(b, 32, stride=32), :].astype(BF16)

    def outer_of(c_, x_):
        ya, _ = chunk_at(q, x_, zh)
        yb, _ = chunk_at(q, x_, (zh + 1) % 4)
        yc, _ = chunk_at(q, x_, (zh + 2) % 4)
        y2 = jnp.where(yb == ya, yc, yb)
        ga, gb = c_ * 8 + ya, c_ * 8 + y2
        rows = jnp.concatenate([left[ga], left[gb]], axis=0)

        @pl.loop(0, 4)
        def _(t):
            part = dot_t(right_p[pl.ds(pl.multiple_of(t * 256, 256), 256), :], rows).astype(BF16)
            for b in range(8):
                lanes = pl.ds(pl.multiple_of(t * 1024 + b * 128, 128), 128)
                outer[ga, :, lanes] = part[b * 32:(b + 1) * 32, 0:128]
                outer[gb, :, lanes] = part[b * 32:(b + 1) * 32, 128:256]

    def pair_of(c_):
        @pl.loop(0, 2)
        def _(t):
            first = c_ * 8 + t * 4
            rows = outer[pl.ds(first, 4)].reshape(128, 4096)
            total = dot(rows, bd[...]) * (1.0 / 256.0)
            for g in range(4):
                for i in range(4):
                    pair[(first + g) * 4 + i] = (
                        total[g * 32:(g + 1) * 32, i * 128:(i + 1) * 128] + bc[...]
                    ).astype(BF16)

    outer_of(c, x)
    for k in (1, 3, 2):
        xo = (x + 4 - k) % 4
        for i in range(4):
            cy, czl = chunk_at(q, xo, (zh + 4 - i) % 4)
            here = left_chunk(c, cy, czl)
            send(here, here, lx_send.at[i * 3 + k - 1], lx_recv.at[i * 3 + k - 1], x_dev[k]).wait_recv()
            go(here, here, lc_send.at[4 + (k - 1) * 4 + i], lc_recv.at[4 + (k - 1) * 4 + i], core_dev)
        outer_of(c, xo)
    pair_of(c)
    for k in (0, 1, 3, 2):
        xo = (x + 4 - k) % 4
        for i in range(4):
            cy, czl = chunk_at(q, xo, (zh + 4 - i) % 4)
            there = left_chunk(1 - c, cy, czl)
            slot = i if k == 0 else 4 + (k - 1) * 4 + i
            send(there, there, lc_send.at[slot], lc_recv.at[slot], core_dev).wait_recv()
        outer_of(1 - c, xo)
    pair_of(1 - c)

    out1 = pltpu.make_async_copy(pair, pair_out, load_sem.at[0])
    out1.start()
    for copy in back:
        copy.wait_recv()
    out2 = pltpu.make_async_copy(upd_all, upd_out, load_sem.at[1])
    out2.start()
    for k in order:
        turn[k].wait_send()
    for copy in sent:
        copy.wait_send()
    out1.wait()
    out2.wait()


def local(
    alignment_embedding, heed_layer_gain, heed_layer_shift, probe_weights, lookup_weights,
    content_weights, sigmoid_weights, sigmoid_shift, final_weights, final_shift,
    tensor_layer_gain, tensor_layer_shift, first_factor_weights, second_factor_weights,
    couple_weights, couple_shift,
):
    row = lambda a: a.reshape(1, -1)
    hbm = pl.BlockSpec(memory_space=pl.ANY)
    vmem = pl.BlockSpec(memory_space=pltpu.VMEM)
    sem = pltpu.SemaphoreType.DMA
    buf = lambda *shape: pltpu.VMEM(shape, BF16)
    upd, pair = pl.pallas_call(
        kernel,
        out_shape=(
            jax.ShapeDtypeStruct((32, 16, 256), BF16),
            jax.ShapeDtypeStruct((64, 32, 128), BF16),
        ),
        in_specs=[hbm, vmem, vmem, hbm, hbm, hbm, hbm, vmem, hbm, vmem, vmem, vmem, hbm, hbm, hbm, vmem],
        out_specs=(hbm, hbm),
        scratch_shapes=[
            buf(16, 32, 256), pltpu.VMEM((2, 512, 128), F32), buf(32, 16, 256), buf(2, 256, 256),
            buf(256, 256), buf(256, 256), buf(256, 256), buf(256, 256), buf(256, 256),
            buf(256, 32), buf(256, 32), buf(1024, 128), pltpu.VMEM((1024, 128), F32),
            buf(768, 256), buf(64, 256), buf(8, 48, 256), pltpu.VMEM((256, 256), F32), buf(4096, 512),
            buf(2, 256, 256), buf(32, 16, 256), buf(64, 256), buf(64, 256), buf(16, 128, 256),
            buf(16, 64, 256), pltpu.VMEM((2, 1024, 128), F32), buf(1024, 256), buf(16, 32, 4096),
            buf(64, 32, 128),
            sem((9,)), sem((16,)), sem((16,)), sem((16,)), sem((16,)), sem((1,)), sem((1,)),
            sem((8,)), sem((8,)), sem((8,)), sem((8,)), sem((3,)), sem((3,)),
            sem((12,)), sem((12,)), sem((16,)), sem((16,)),
        ],
        compiler_params=pltpu.CompilerParams(
            collective_id=0, has_side_effects=True, vmem_limit_bytes=40 * 2**20
        ),
        name="evoformer",
    )(
        alignment_embedding, row(heed_layer_gain), row(heed_layer_shift), probe_weights,
        lookup_weights, content_weights, sigmoid_weights, sigmoid_shift.reshape(-1, 1),
        final_weights, row(final_shift), row(tensor_layer_gain), row(tensor_layer_shift),
        first_factor_weights, second_factor_weights, couple_weights, row(couple_shift),
    )
    return upd.transpose(1, 0, 2), pair


def solution(mesh):
    return jax.shard_map(
        local,
        mesh=mesh,
        in_specs=(P("seq", "res", None),) + (P(),) * 15,
        out_specs=(P("seq", "res", None), P("seq", "res", None)),
        check_vma=False,
    )
```

time: 500 us -> 70.7 us (0.14)
  the two profiles are of different devices: /device:TPU:1 before, /device:TPU:12 now
where the time goes in v1:
time: 70.7 us; the launch traced here: 70.4 us
  Pallas kernels  60 us (85%)
  local copies, waits for them, and re-layouts  9.63 us (14%)
  between operations  0.77 us (1%)
    pallas_call x1, Pallas kernels, local(): pl.pallas_call(kernel, out_shape=(jax.ShapeDtypeStruct((32, 16, 256), BF1...  60 us
    unnamed x30, local copies, waits for them, and re-layouts  8.79 us

profile of v1, /device:TPU:12, one launch (start us, length us, event | category | flops | bytes accessed | tf_op | source)
XLA Modules:
  0.0 70.4 jit_solution(5588783493815014358)
XLA Ops:
  0.6 0.0 copy-start
  0.6 0.9 %copy.22.w1_hbm = bf16[256,32]{1,0:T(8,128)(2,1)S(1)} copy(bf16[256,32]{0,1:T(8,128)(2,1)} %param.28) | data formatting | bytes 32768 | tf_op args[12]
  1.5 0.8 %copy.23.w2_hbm = bf16[256,32]{1,0:T(8,128)(2,1)S(1)} copy(bf16[256,32]{0,1:T(8,128)(2,1)} %param.29) | data formatting | bytes 32768 | tf_op args[13]
  2.4 0.0 copy-start.7
  2.4 0.0 copy-start.8
  2.4 0.0 copy-start.9
  2.4 0.0 copy-start.10
  2.4 0.0 copy-start.11
  2.4 0.0 copy-start.12
  2.4 0.8 %copy.21.bg = f32[256,1]{1,0:T(8,128)S(1)} copy(f32[256,1]{0,1:T(1,128)} %bitcast.15) | data formatting | bytes 2048 | tf_op jit(solution)/shard_map/reshape | solution.py:334
  3.3 0.0 copy-done
  3.3 0.0 copy-done.7
  3.3 0.0 copy-done.8
  3.3 0.0 copy-done.9
  3.3 0.0 copy-done.10
  3.3 0.0 copy-done.11
  3.3 0.0 copy-done.12
  3.3 0.0 copy-start.1
  3.3 0.9 %copy-done.1 = bf16[1024,128]{1,0:T(8,128)(2,1)S(1)} copy-done((bf16[1024,128]{1,0:T(8,128)(2,1)S(1)}, bf16[1024,128]{1,0:T(8,128)(2,1)}, u32[]{:S(2)}) %copy-start.1) | copy-done | bytes 262168
  4.3 0.0 copy-start.2
  4.3 0.9 %copy-done.2 = bf16[256,256]{1,0:T(8,128)(2,1)S(1)} copy-done((bf16[256,256]{1,0:T(8,128)(2,1)S(1)}, bf16[256,256]{1,0:T(8,128)(2,1)}, u32[]{:S(2)}) %copy-start.2) | copy-done | bytes 131096
  5.2 0.0 copy-start.3
  5.2 0.9 %copy-done.3 = bf16[256,256]{1,0:T(8,128)(2,1)S(1)} copy-done((bf16[256,256]{1,0:T(8,128)(2,1)S(1)}, bf16[256,256]{1,0:T(8,128)(2,1)}, u32[]{:S(2)}) %copy-start.3) | copy-done | bytes 131096
  6.1 0.0 copy-start.4
  6.1 0.9 %copy-done.4 = bf16[256,256]{1,0:T(8,128)(2,1)S(1)} copy-done((bf16[256,256]{1,0:T(8,128)(2,1)S(1)}, bf16[256,256]{1,0:T(8,128)(2,1)}, u32[]{:S(2)}) %copy-start.4) | copy-done | bytes 131096
  7.0 0.0 copy-start.5
  7.0 0.9 %copy-done.5 = bf16[256,256]{1,0:T(8,128)(2,1)S(1)} copy-done((bf16[256,256]{1,0:T(8,128)(2,1)S(1)}, bf16[256,256]{1,0:T(8,128)(2,1)}, u32[]{:S(2)}) %copy-start.5) | copy-done | bytes 131096
  7.9 0.0 copy-start.6
  7.9 0.9 %copy-done.6 = bf16[256,256]{1,0:T(8,128)(2,1)S(1)} copy-done((bf16[256,256]{1,0:T(8,128)(2,1)S(1)}, bf16[256,256]{1,0:T(8,128)(2,1)}, u32[]{:S(2)}) %copy-start.6) | copy-done | bytes 131096
  8.8 60.0 %evoformer.1 = (bf16[32,16,256]{2,1,0:T(8,128)(2,1)S(1)}, bf16[64,32,128]{2,1,0:T(8,128)(2,1)S(1)}) custom-call(bf16[16,32,256]{2,1,0:T(8,128)(2,1)S(1)} %copy-done, f32[1,256]{1,0:T(1,128)S(1)} %bitcast.9, f32[1,256]{1,0:T(1,128)S(1)} %bitcast.10, bf16[256,256]{1,0:T(8,128)(2,1)S(1)} %copy-done.2, bf16[256,256]{1,0:T(8,128)(2,1)S(1)} %copy-done.3, ...), custom_call_target="tpu_custom_call" | custom-call | tf_op jit(solution)/shard_map/evoformer/pallas_call | solution.py:308
  68.8 0.8 %copy.24 = bf16[16,32,256]{2,1,0:T(8,128)(2,1)} copy(bf16[16,32,256]{2,0,1:T(8,128)(2,1)S(1)} %bitcast.8) | data formatting | bytes 524288
  69.6 0.8 %copy.26 = bf16[64,32,128]{2,1,0:T(8,128)(2,1)} copy(bf16[64,32,128]{2,1,0:T(8,128)(2,1)S(1)} %get-tuple-element.13) | data formatting | bytes 1048576
Async XLA Ops:
  0.6 2.6 %copy-start = (bf16[16,32,256]{2,1,0:T(8,128)(2,1)S(1)}, bf16[16,32,256]{2,1,0:T(8,128)(2,1)}, u32[]{:S(2)}) copy-start(bf16[16,32,256]{2,1,0:T(8,128)(2,1)} %x_hbm.1) | copy-start | bytes 786436
  2.4 0.9 %copy-start.7 = (f32[256]{0:T(256)S(1)}, f32[256]{0:T(256)}, u32[]{:S(2)}) copy-start(f32[256]{0:T(256)} %param.17) | copy-start | bytes 3076
  2.4 0.9 %copy-start.8 = (f32[256]{0:T(256)S(1)}, f32[256]{0:T(256)}, u32[]{:S(2)}) copy-start(f32[256]{0:T(256)} %param.18) | copy-start | bytes 3076
  2.4 0.9 %copy-start.9 = (f32[256]{0:T(256)S(1)}, f32[256]{0:T(256)}, u32[]{:S(2)}) copy-start(f32[256]{0:T(256)} %param.25) | copy-start | bytes 3076
  2.4 0.9 %copy-start.10 = (f32[256]{0:T(256)S(1)}, f32[256]{0:T(256)}, u32[]{:S(2)}) copy-start(f32[256]{0:T(256)} %param.26) | copy-start | bytes 3076
  2.4 0.9 %copy-start.11 = (f32[256]{0:T(256)S(1)}, f32[256]{0:T(256)}, u32[]{:S(2)}) copy-start(f32[256]{0:T(256)} %param.27) | copy-start | bytes 3076
  2.4 0.9 %copy-start.12 = (f32[128]{0:T(128)S(1)}, f32[128]{0:T(128)}, u32[]{:S(2)}) copy-start(f32[128]{0:T(128)} %param.31) | copy-start | bytes 1540
  3.3 1.0 %copy-start.1 = (bf16[1024,128]{1,0:T(8,128)(2,1)S(1)}, bf16[1024,128]{1,0:T(8,128)(2,1)}, u32[]{:S(2)}) copy-start(bf16[1024,128]{1,0:T(8,128)(2,1)} %wc_hbm.1) | copy-start | bytes 786436
  4.3 0.9 %copy-start.2 = (bf16[256,256]{1,0:T(8,128)(2,1)S(1)}, bf16[256,256]{1,0:T(8,128)(2,1)}, u32[]{:S(2)}) copy-start(bf16[256,256]{1,0:T(8,128)(2,1)} %wq_hbm.1) | copy-start | bytes 393220
  5.2 0.9 %copy-start.3 = (bf16[256,256]{1,0:T(8,128)(2,1)S(1)}, bf16[256,256]{1,0:T(8,128)(2,1)}, u32[]{:S(2)}) copy-start(bf16[256,256]{1,0:T(8,128)(2,1)} %wk_hbm.1) | copy-start | bytes 393220
  6.1 0.9 %copy-start.4 = (bf16[256,256]{1,0:T(8,128)(2,1)S(1)}, bf16[256,256]{1,0:T(8,128)(2,1)}, u32[]{:S(2)}) copy-start(bf16[256,256]{1,0:T(8,128)(2,1)} %wv_hbm.1) | copy-start | bytes 393220
  7.0 0.9 %copy-start.5 = (bf16[256,256]{1,0:T(8,128)(2,1)S(1)}, bf16[256,256]{1,0:T(8,128)(2,1)}, u32[]{:S(2)}) copy-start(bf16[256,256]{1,0:T(8,128)(2,1)} %wg_hbm.1) | copy-start | bytes 393220
  7.9 0.9 %copy-start.6 = (bf16[256,256]{1,0:T(8,128)(2,1)S(1)}, bf16[256,256]{1,0:T(8,128)(2,1)}, u32[]{:S(2)}) copy-start(bf16[256,256]{1,0:T(8,128)(2,1)} %wf_hbm.1) | copy-start | bytes 393220

commit v2 on v1

v2 whole, which is shorter than its diff:
```python
import functools

import jax
import jax.numpy as jnp
from jax import lax
from jax.experimental import pallas as pl
from jax.experimental.pallas import tpu as pltpu
from jax.sharding import PartitionSpec as P

HEADS = 8
WIDTH = 32
BF16 = jnp.bfloat16
F32 = jnp.float32
MESH = pl.DeviceIdType.MESH
SPREAD = (4, 5, 3, 6, 2, 7, 1)
SCALE = 1.4426950408889634 / 32.0**0.5


def norm_rows(values, scale, offset):
    center = values - jnp.mean(values, axis=-1, keepdims=True)
    spread = jnp.mean(center * center, axis=-1, keepdims=True)
    return center * lax.rsqrt(spread + 1e-05) * scale + offset


def dot(a, b):
    return jnp.dot(a, b, preferred_element_type=F32)


def dot_t(a, b):
    return lax.dot_general(a, b, (((1,), (1,)), ((), ())), preferred_element_type=F32)


def relay_of(p, y, zl):
    x, zh = p // 4, p % 4
    y_to, zl_to = p // 2, p % 2
    k = (y - y_to + 12) % 8
    dx = (2 * (k // 4) + 3 * (k % 2)) % 4
    far = ((k + 2) // 4) % 2
    e = (zl + zl_to) % 2
    s = 2 * zl_to - 1
    dz = (1 - e) * far * s + e * (far * 2 - (1 - far) * s)
    return (x + dx) % 4, (zh + dz + 8) % 4


def chunk_at(p, x, zh):
    x0, zh0 = p // 4, p % 4
    zl_to = p % 2
    s = 2 * zl_to - 1
    w = (x0 - x + 4) % 4
    u = ((zh - zh0 + 4) * (s + 4)) % 4
    e = u // 2
    far = ((u + 1) // 2) % 2
    k = w + (1 - far) * 4 * (w // 2) + 2 * far
    return (p // 2 + k + 4) % 8, (e + zl_to) % 2


def kernel(
    x_hbm, gain1_hbm, shift1_hbm, wq_hbm, wk_hbm, wv_hbm, wg_hbm, bg_hbm, wf_hbm, bf_hbm, gain2_hbm,
    shift2_hbm, w1_hbm, w2_hbm, wc_hbm, bc_hbm,
    upd_out, pair_out,
    xv, x32, xt, xg, gain1, shift1, bg, bf, gain2, shift2, bc, wq, wk, wv, wg, wf, w12t, wc, w32,
    wt, bg_t, vtx, gated_t, bd,
    upd, upd_all, upd_v, lt, rt, left, right, r32, right_p, outer, pair,
    load_sem, a_send, a_recv, u_send, u_recv, p_send, p_recv, ry_send, ry_recv, rz_send, rz_recv,
    lz_send, lz_recv, lx_send, lx_recv, lc_send, lc_recv,
):
    q = lax.axis_index("seq")
    r = lax.axis_index("res")
    y, zl = q // 2, q % 2
    x, zh, c = r // 8, (r // 2) % 4, r % 2
    plane = r // 2

    def res(x_, zh_, c_):
        return (x_ * 4 + zh_) * 2 + c_

    sent = []

    def copy_to(dev, src, dst, ss, rs, i):
        return pltpu.make_async_remote_copy(
            src_ref=src, dst_ref=dst, send_sem=ss.at[i], recv_sem=rs.at[i], device_id=dev,
            device_id_type=MESH,
        )

    def go(*args):
        copy = copy_to(*args)
        copy.start()
        sent.append(copy)
        return copy

    seq_dev = [((q + k) % 16, r) for k in range(16)]
    y_dev = [(((y + k) % 8) * 2 + zl, r) for k in range(8)]
    zl_dev = (y * 2 + 1 - zl, r)
    zh_dev = [(q, res(x, (zh + k) % 4, c)) for k in range(4)]
    x_dev = [(q, res((x + k) % 4, zh, c)) for k in range(4)]
    core_dev = (q, res(x, zh, 1 - c))
    relay_x, relay_zh = relay_of(plane, y, zl)
    relay_dev = (plane, res(relay_x, relay_zh, c))
    source = [[chunk_at(q, (x + 4 - i) % 4, (zh + 4 - j) % 4) for j in range(4)] for i in range(4)]
    held = [[source[i][j][0] * 2 + source[i][j][1] for j in range(4)] for i in range(4)]
    from_dev = (held[0][0], 2 * q + c)

    barrier = pltpu.get_barrier_semaphore()
    greet = seq_dev[1:] + zh_dev[1:] + x_dev[1:] + [core_dev, from_dev]
    for dev in greet:
        pl.semaphore_signal(barrier, inc=1, device_id=dev, device_id_type=MESH)

    loads = [
        pltpu.make_async_copy(a, b, load_sem.at[i])
        for i, (a, b) in enumerate(
            [(x_hbm, xv), (wc_hbm, wc), (wq_hbm, wq), (wk_hbm, wk), (wv_hbm, wv), (wg_hbm, wg),
             (wf_hbm, wf), (w1_hbm, w12t.at[0:32]), (w2_hbm, w12t.at[32:64]), (gain1_hbm, gain1),
             (shift1_hbm, shift1), (bg_hbm, bg), (bf_hbm, bf), (gain2_hbm, gain2),
             (shift2_hbm, shift2), (bc_hbm, bc)]
        )
    ]
    for copy in loads:
        copy.start()

    loads[0].wait()
    for i in range(16):
        for half in range(2):
            x32[half, i * 32:(i + 1) * 32, :] = xv[i, :, half * 128:(half + 1) * 128].astype(F32)
    for i in range(32):
        for half in range(2):
            xt[i, :, half * 128:(half + 1) * 128] = x32[half, pl.ds(i, 16, stride=32), :].astype(BF16)

    mine = pl.ds(pl.multiple_of(q * 16, 16), 16)
    for m in range(2):
        xg[m, mine, :] = xt[2 * q + m]

    pl.semaphore_wait(barrier, len(greet))
    order = (8, 7, 9, 6, 10, 5, 11, 4, 12, 3, 13, 2, 14, 1, 15)
    turn = [
        [go(seq_dev[k], xt.at[2 * seq_dev[k][0] + m], xg.at[m, mine, :], a_send, a_recv, m * 16 + k)
         for k in order]
        for m in range(2)
    ]

    for copy in loads[1:]:
        copy.wait()
    wt[0:256, :] = wq[...].astype(F32).T.astype(BF16)
    wt[256:512, :] = wv[...].astype(F32).T.astype(BF16)
    wt[512:768, :] = wg[...].astype(F32).T.astype(BF16)
    bg_t[...] = jnp.broadcast_to(bg[...], (128, 256)).T
    vtx[:, 32:48, :] = jnp.ones((HEADS, 16, 256), BF16)
    w32[...] = wc[...].astype(F32)

    @pl.loop(0, 32)
    def _(b):
        block = w32[pl.ds(b, 32, stride=32), :].astype(BF16)
        zero = jnp.zeros((32, 128), BF16)
        for i in range(4):
            rows = pl.ds(pl.multiple_of(b * 128 + i * 32, 32), 32)
            for j in range(4):
                bd[rows, j * 128:(j + 1) * 128] = block if i == j else zero

    def attend(m):
        given = xg[m].astype(F32)
        normed = norm_rows(given, gain1[...], shift1[...]).astype(BF16)
        keys = dot(normed, wk[...]).astype(BF16)
        qvg = dot_t(wt[...], normed)
        queries_t = qvg[0:256].astype(BF16)
        vtx[:, 0:32, :] = qvg[256:512].astype(BF16).reshape(HEADS, WIDTH, 256)
        gate_t = 1.0 / (1.0 + jnp.exp(-(qvg[512:768] + bg_t[:, 0:1])))
        for h in range(HEADS):
            span = slice(h * WIDTH, (h + 1) * WIDTH)
            scores = dot(keys[:, span], queries_t[span, :])
            top = jnp.max(scores, axis=0, keepdims=True)
            weights = jnp.exp2((scores - top) * SCALE).astype(BF16)
            mixed = dot(vtx[h], weights)
            gated_t[span, :] = mixed[0:32] * (1.0 / mixed[32:33]) * gate_t[span, :]
        gated = gated_t[...].T.astype(BF16)
        attended = (dot(gated, wf[...]) + bf[...]).astype(BF16)
        updated = (given + attended.astype(F32)).astype(BF16)
        upd[m] = updated
        outer_normed = norm_rows(updated.astype(F32), gain2[...], shift2[...]).astype(BF16)
        both = dot_t(w12t[...], outer_normed).astype(BF16)
        lt[m] = both[0:32]
        rt[m] = both[32:64]

    def slot(c_, q_, m):
        return left.at[(c_ * 16 + q_) * 2 + m]

    relay, along, across, back = [], [], [], []
    for m in range(2):
        for copy in turn[m][::-1]:
            copy.wait_recv()
        attend(m)
        relay.append(go(relay_dev, lt.at[m], slot(c, q, m), p_send, p_recv, m))
        here = right.at[2 * q + m]
        across.append(go(zl_dev, rt.at[m], here, rz_send, rz_recv, m * 8))
        along.append(
            {k: go(y_dev[k], rt.at[m], here, ry_send, ry_recv, m * 8 + k) for k in SPREAD}
        )
        right[2 * q + m] = rt[m]
        for k in order:
            rows = pl.ds(pl.multiple_of(seq_dev[k][0] * 16, 16), 16)
            back.append(
                go(seq_dev[k], upd.at[m, rows, :], upd_all.at[2 * q + m], u_send, u_recv, m * 16 + k)
            )
        upd_all[2 * q + m] = upd[m, mine, :]

    def pass_on(j, m):
        here = slot(c, held[0][j], m)
        for k in (2, 1, 3):
            go(x_dev[k], here, here, lx_send, lx_recv, m * 12 + j * 3 + k - 1)
        go(core_dev, here, here, lc_send, lc_recv, m * 16 + j)

    z_left = []
    for m in range(2):
        relay[m].wait_recv()
        here = slot(c, held[0][0], m)
        z_left.append({k: go(zh_dev[k], here, here, lz_send, lz_recv, m * 3 + k - 1) for k in (2, 1, 3)})
        pass_on(0, m)
        for k in SPREAD[::-1]:
            along[m][k].wait_recv()
            here = right.at[(((y + 8 - k) % 8) * 2 + zl) * 2 + m]
            across.append(go(zl_dev, here, here, rz_send, rz_recv, m * 8 + k))
    for m in range(2):
        for k in (1, 3, 2):
            z_left[m][k].wait_recv()
            pass_on(k, m)

    for copy in across:
        copy.wait_recv()

    for i in range(32):
        for half in range(2):
            r32[half, i * 32:(i + 1) * 32, :] = right[i, :, half * 128:(half + 1) * 128].astype(F32)
    for b in range(32):
        for half in range(2):
            right_p[b * 32:(b + 1) * 32, half * 128:(half + 1) * 128] = r32[
                half, pl.ds(b, 32, stride=32), :
            ].astype(BF16)

    def outer_of(c_, m, pick):
        at = [(c_ * 16 + held[i][j]) * 2 + m for i, j in pick]
        rows = jnp.concatenate([left[n] for n in at], axis=0)
        for t in range(4):
            part = dot_t(right_p[t * 256:(t + 1) * 256, :], rows).astype(BF16)
            for b in range(8):
                lanes = slice(t * 1024 + b * 128, t * 1024 + (b + 1) * 128)
                for g in range(2):
                    outer[group_no[0] * 2 + g, :, lanes] = part[b * 32:(b + 1) * 32, g * 128:(g + 1) * 128]
        owner.extend(c_ * 32 + 2 * held[i][j] + m for i, j in pick)
        group_no[0] += 1

    group_no, owner = [0], []

    def pair_of(first, count):
        rows = outer[first:first + count].reshape(count * 32, 4096)
        total = dot(rows, bd[...]) * (1.0 / 256.0)
        for g in range(count):
            for i in range(4):
                pair[owner[(first + g) * 4 + i]] = (
                    total[g * 32:(g + 1) * 32, i * 128:(i + 1) * 128] + bc[...]
                ).astype(BF16)

    FIRST = [(i, j) for j in (0, 1) for i in range(4)]
    SECOND = [(i, j) for j in (3, 2) for i in range(4)]

    def from_x(m):
        for j in (0, 1, 3, 2):
            for k in (1, 3, 2):
                here = slot(c, held[k][j], m)
                copy_to(x_dev[k], here, here, lx_send, lx_recv, m * 12 + j * 3 + k - 1).wait_recv()
                go(core_dev, here, here, lc_send, lc_recv, m * 16 + k * 4 + j)

    def from_core(m, pick):
        for k, j in pick:
            there = slot(1 - c, held[k][j], m)
            copy_to(core_dev, there, there, lc_send, lc_recv, m * 16 + k * 4 + j).wait_recv()

    from_x(0)
    outer_of(c, 0, FIRST)
    outer_of(c, 0, SECOND)

    for copy in back:
        copy.wait_recv()
    for i in range(32):
        for half in range(2):
            x32[half, i * 16:(i + 1) * 16, :] = upd_all[i, :, half * 128:(half + 1) * 128].astype(F32)
    for i in range(16):
        for half in range(2):
            upd_v[i, :, half * 128:(half + 1) * 128] = x32[half, pl.ds(i, 32, stride=16), :].astype(BF16)
    out1 = pltpu.make_async_copy(upd_v, upd_out, load_sem.at[0])
    out1.start()

    from_core(0, FIRST)
    outer_of(1 - c, 0, FIRST)
    from_core(0, SECOND)
    outer_of(1 - c, 0, SECOND)
    from_x(1)
    pair_of(0, 8)
    outer_of(c, 1, FIRST)
    outer_of(c, 1, SECOND)
    pair_of(8, 4)
    from_core(1, FIRST)
    outer_of(1 - c, 1, FIRST)
    from_core(1, SECOND)
    outer_of(1 - c, 1, SECOND)
    pair_of(12, 4)

    out2 = pltpu.make_async_copy(pair, pair_out, load_sem.at[1])
    out2.start()
    for copy in sent:
        copy.wait_send()
    out1.wait()
    out2.wait()


def local(
    alignment_embedding, heed_layer_gain, heed_layer_shift, probe_weights, lookup_weights,
    content_weights, sigmoid_weights, sigmoid_shift, final_weights, final_shift,
    tensor_layer_gain, tensor_layer_shift, first_factor_weights, second_factor_weights,
    couple_weights, couple_shift,
):
    row = lambda a: a.reshape(1, -1)
    hbm = pl.BlockSpec(memory_space=pltpu.HBM)
    sem = pltpu.SemaphoreType.DMA
    buf = lambda *shape: pltpu.VMEM(shape, BF16)
    line = lambda n: pltpu.VMEM((1, n), F32)
    upd, pair = pl.pallas_call(
        kernel,
        out_shape=(
            jax.ShapeDtypeStruct((16, 32, 256), BF16),
            jax.ShapeDtypeStruct((64, 32, 128), BF16),
        ),
        in_specs=[hbm] * 16,
        out_specs=(hbm, hbm),
        scratch_shapes=[
            buf(16, 32, 256), pltpu.VMEM((2, 512, 128), F32), buf(32, 16, 256), buf(2, 256, 256),
            line(256), line(256), line(256), line(256), line(256), line(256), line(128),
            buf(256, 256), buf(256, 256), buf(256, 256), buf(256, 256), buf(256, 256),
            buf(64, 256), buf(1024, 128), pltpu.VMEM((1024, 128), F32),
            buf(768, 256), pltpu.VMEM((256, 128), F32), buf(8, 48, 256), pltpu.VMEM((256, 256), F32), buf(4096, 512),
            buf(2, 256, 256), buf(32, 16, 256), buf(16, 32, 256), buf(2, 32, 256), buf(2, 32, 256),
            buf(64, 32, 256), buf(32, 32, 256), pltpu.VMEM((2, 1024, 128), F32), buf(1024, 256), buf(16, 32, 4096),
            buf(64, 32, 128),
            sem((16,)), sem((32,)), sem((32,)), sem((32,)), sem((32,)), sem((2,)), sem((2,)),
            sem((16,)), sem((16,)), sem((16,)), sem((16,)), sem((6,)), sem((6,)),
            sem((24,)), sem((24,)), sem((32,)), sem((32,)),
        ],
        compiler_params=pltpu.CompilerParams(
            collective_id=0, has_side_effects=True, vmem_limit_bytes=60 * 2**20
        ),
        name="evoformer",
    )(
        alignment_embedding, row(heed_layer_gain), row(heed_layer_shift), probe_weights,
        lookup_weights, content_weights, sigmoid_weights, row(sigmoid_shift),
        final_weights, row(final_shift), row(tensor_layer_gain), row(tensor_layer_shift),
        first_factor_weights.T, second_factor_weights.T, couple_weights, row(couple_shift),
    )
    return upd, pair


def solution(mesh):
    return jax.shard_map(
        local,
        mesh=mesh,
        in_specs=(P("seq", "res", None),) + (P(),) * 15,
        out_specs=(P("seq", "res", None), P("seq", "res", None)),
        check_vma=False,
    )
```

time: 70.7 us -> 56.2 us (0.79)
  the two profiles are of different devices: /device:TPU:12 before, /device:TPU:1 now
where the time goes in v2:
time: 56.2 us; the launch traced here: 56 us
  Pallas kernels  52.8 us (94%)
  local copies, waits for them, and re-layouts  2.52 us (4%)
  between operations  0.65 us (1%)
    pallas_call x1, Pallas kernels, local(): pl.pallas_call(kernel, out_shape=(jax.ShapeDtypeStruct((16, 32, 256), BF1...  52.8 us
    unnamed x4, local copies, waits for them, and re-layouts  2.52 us

profile of v2, /device:TPU:1, one launch (start us, length us, event | category | flops | bytes accessed | tf_op | source)
XLA Modules:
  0.0 56.0 jit_solution(8031424917508579167)
XLA Ops:
  0.6 52.8 %evoformer.1 = (bf16[16,32,256]{2,1,0:T(8,128)(2,1)}, bf16[64,32,128]{2,1,0:T(8,128)(2,1)}) custom-call(bf16[16,32,256]{2,1,0:T(8,128)(2,1)} %x_hbm.1, f32[1,256]{1,0:T(1,128)} %bitcast.11, f32[1,256]{1,0:T(1,128)} %bitcast.12, bf16[256,256]{1,0:T(8,128)(2,1)} %wq_hbm.1, bf16[256,256]{1,0:T(8,128)(2,1)} %wk_hbm.1, bf16[256,256]{1,0:T(8,128)(2,1)} %wv_hbm.1, ...), custom_call_target="tpu_custom_call" | custom-call | tf_op jit(solution)/shard_map/evoformer/pallas_call | solution.py:323
  53.5 0.0 copy-start
  53.5 1.7 %copy.20 = bf16[16,32,256]{2,1,0:T(8,128)(2,1)} copy(bf16[16,32,256]{2,1,0:T(8,128)(2,1)} %get-tuple-element.4) | data formatting | bytes 524288
  55.2 0.0 copy-done
  55.2 0.8 %copy.21 = bf16[64,32,128]{2,1,0:T(8,128)(2,1)} copy(bf16[64,32,128]{2,1,0:T(8,128)(2,1)S(1)} %copy-done) | data formatting | bytes 1048576
Async XLA Ops:
  53.5 1.7 %copy-start = (bf16[64,32,128]{2,1,0:T(8,128)(2,1)S(1)}, bf16[64,32,128]{2,1,0:T(8,128)(2,1)}, u32[]{:S(2)}) copy-start(bf16[64,32,128]{2,1,0:T(8,128)(2,1)} %get-tuple-element.5) | copy-start | bytes 1572868

commit v3 on v2

--- a/solution.py
+++ b/solution.py
@@ -57,10 +57,10 @@
 def kernel(
     x_hbm, gain1_hbm, shift1_hbm, wq_hbm, wk_hbm, wv_hbm, wg_hbm, bg_hbm, wf_hbm, bf_hbm, gain2_hbm,
     shift2_hbm, w1_hbm, w2_hbm, wc_hbm, bc_hbm,
-    upd_out, pair_out,
+    upd_v, pair,
     xv, x32, xt, xg, gain1, shift1, bg, bf, gain2, shift2, bc, wq, wk, wv, wg, wf, w12t, wc, w32,
-    wt, bg_t, vtx, gated_t, bd,
-    upd, upd_all, upd_v, lt, rt, left, right, r32, right_p, outer, pair,
+    wt, bg_t, vtx, weights, gated_t, bd,
+    upd, upd_all, lt, rt, left, right, r32, right_p, outer,
     load_sem, a_send, a_recv, u_send, u_recv, p_send, p_recv, ry_send, ry_recv, rz_send, rz_recv,
     lz_send, lz_recv, lx_send, lx_recv, lc_send, lc_recv,
 ):
@@ -163,11 +163,20 @@
         vtx[:, 0:32, :] = qvg[256:512].astype(BF16).reshape(HEADS, WIDTH, 256)
         gate_t = 1.0 / (1.0 + jnp.exp(-(qvg[512:768] + bg_t[:, 0:1])))
         for h in range(HEADS):
+            group, place = h // 4, h % 4
+            padded = jnp.concatenate(
+                [
+                    queries_t[h * WIDTH:(h + 1) * WIDTH, :] if i == place else jnp.zeros((WIDTH, 256), BF16)
+                    for i in range(4)
+                ],
+                axis=0,
+            )
+            scores = dot(keys[:, group * 128:(group + 1) * 128], padded)
+            top = jnp.max(scores, axis=0, keepdims=True)
+            weights[h] = jnp.exp2((scores - top) * SCALE).astype(BF16)
+        for h in range(HEADS):
             span = slice(h * WIDTH, (h + 1) * WIDTH)
-            scores = dot(keys[:, span], queries_t[span, :])
-            top = jnp.max(scores, axis=0, keepdims=True)
-            weights = jnp.exp2((scores - top) * SCALE).astype(BF16)
-            mixed = dot(vtx[h], weights)
+            mixed = dot(vtx[h], weights[h])
             gated_t[span, :] = mixed[0:32] * (1.0 / mixed[32:33]) * gate_t[span, :]
         gated = gated_t[...].T.astype(BF16)
         attended = (dot(gated, wf[...]) + bf[...]).astype(BF16)
@@ -193,12 +202,14 @@
             {k: go(y_dev[k], rt.at[m], here, ry_send, ry_recv, m * 8 + k) for k in SPREAD}
         )
         right[2 * q + m] = rt[m]
+        upd_all[2 * q + m] = upd[m, mine, :]
+
+    def send_back(m):
         for k in order:
             rows = pl.ds(pl.multiple_of(seq_dev[k][0] * 16, 16), 16)
             back.append(
                 go(seq_dev[k], upd.at[m, rows, :], upd_all.at[2 * q + m], u_send, u_recv, m * 16 + k)
             )
-        upd_all[2 * q + m] = upd[m, mine, :]
 
     def pass_on(j, m):
         here = slot(c, held[0][j], m)
@@ -216,22 +227,12 @@
             along[m][k].wait_recv()
             here = right.at[(((y + 8 - k) % 8) * 2 + zl) * 2 + m]
             across.append(go(zl_dev, here, here, rz_send, rz_recv, m * 8 + k))
+    send_back(0)
+    send_back(1)
     for m in range(2):
         for k in (1, 3, 2):
             z_left[m][k].wait_recv()
             pass_on(k, m)
-
-    for copy in across:
-        copy.wait_recv()
-
-    for i in range(32):
-        for half in range(2):
-            r32[half, i * 32:(i + 1) * 32, :] = right[i, :, half * 128:(half + 1) * 128].astype(F32)
-    for b in range(32):
-        for half in range(2):
-            right_p[b * 32:(b + 1) * 32, half * 128:(half + 1) * 128] = r32[
-                half, pl.ds(b, 32, stride=32), :
-            ].astype(BF16)
 
     def outer_of(c_, m, pick):
         at = [(c_ * 16 + held[i][j]) * 2 + m for i, j in pick]
@@ -242,17 +243,17 @@
                 lanes = slice(t * 1024 + b * 128, t * 1024 + (b + 1) * 128)
                 for g in range(2):
                     outer[group_no[0] * 2 + g, :, lanes] = part[b * 32:(b + 1) * 32, g * 128:(g + 1) * 128]
-        owner.extend(c_ * 32 + 2 * held[i][j] + m for i, j in pick)
+        owner.extend(c_ * 16 + held[i][j] for i, j in pick)
         group_no[0] += 1
 
     group_no, owner = [0], []
 
-    def pair_of(first, count):
+    def pair_of(first, count, of):
         rows = outer[first:first + count].reshape(count * 32, 4096)
         total = dot(rows, bd[...]) * (1.0 / 256.0)
         for g in range(count):
             for i in range(4):
-                pair[owner[(first + g) * 4 + i]] = (
+                pair[owner[(first + g) * 4 + i], of] = (
                     total[g * 32:(g + 1) * 32, i * 128:(i + 1) * 128] + bc[...]
                 ).astype(BF16)
 
@@ -272,8 +273,31 @@
             copy_to(core_dev, there, there, lc_send, lc_recv, m * 16 + k * 4 + j).wait_recv()
 
     from_x(0)
+    for copy in across:
+        copy.wait_recv()
+
+    for i in range(32):
+        for half in range(2):
+            r32[half, i * 32:(i + 1) * 32, :] = right[i, :, half * 128:(half + 1) * 128].astype(F32)
+    for b in range(32):
+        for half in range(2):
+            right_p[b * 32:(b + 1) * 32, half * 128:(half + 1) * 128] = r32[
+                half, pl.ds(b, 32, stride=32), :
+            ].astype(BF16)
+
     outer_of(c, 0, FIRST)
     outer_of(c, 0, SECOND)
+    for pick in (FIRST, SECOND):
+        from_core(0, pick)
+        outer_of(1 - c, 0, pick)
+    from_x(1)
+    pair_of(0, 8, 0)
+    outer_of(c, 1, FIRST)
+    outer_of(c, 1, SECOND)
+    for pick in (FIRST, SECOND):
+        from_core(1, pick)
+        outer_of(1 - c, 1, pick)
+    pair_of(8, 8, 1)
 
     for copy in back:
         copy.wait_recv()
@@ -283,30 +307,19 @@
     for i in range(16):
         for half in range(2):
             upd_v[i, :, half * 128:(half + 1) * 128] = x32[half, pl.ds(i, 32, stride=16), :].astype(BF16)
-    out1 = pltpu.make_async_copy(upd_v, upd_out, load_sem.at[0])
-    out1.start()
-
-    from_core(0, FIRST)
-    outer_of(1 - c, 0, FIRST)
-    from_core(0, SECOND)
-    outer_of(1 - c, 0, SECOND)
-    from_x(1)
-    pair_of(0, 8)
-    outer_of(c, 1, FIRST)
-    outer_of(c, 1, SECOND)
-    pair_of(8, 4)
-    from_core(1, FIRST)
-    outer_of(1 - c, 1, FIRST)
-    from_core(1, SECOND)
-    outer_of(1 - c, 1, SECOND)
-    pair_of(12, 4)
-
-    out2 = pltpu.make_async_copy(pair, pair_out, load_sem.at[1])
-    out2.start()
     for copy in sent:
         copy.wait_send()
-    out1.wait()
-    out2.wait()
+
+
+def place(upd, pair, upd_out, pair_out, sems):
+    copies = [
+        pltpu.make_async_copy(pair, pair_out, sems.at[0]),
+        pltpu.make_async_copy(upd, upd_out, sems.at[1]),
+    ]
+    for copy in copies:
+        copy.start()
+    for copy in copies:
+        copy.wait()
 
 
 def local(
@@ -317,41 +330,55 @@
 ):
     row = lambda a: a.reshape(1, -1)
     hbm = pl.BlockSpec(memory_space=pltpu.HBM)
+    vmem = pl.BlockSpec(memory_space=pltpu.VMEM)
+    at_hbm = lambda a: pltpu.with_memory_space_constraint(a, pltpu.HBM)
+    at_vmem = lambda a: pltpu.with_memory_space_constraint(a, pltpu.VMEM)
     sem = pltpu.SemaphoreType.DMA
     buf = lambda *shape: pltpu.VMEM(shape, BF16)
     line = lambda n: pltpu.VMEM((1, n), F32)
     upd, pair = pl.pallas_call(
         kernel,
         out_shape=(
-            jax.ShapeDtypeStruct((16, 32, 256), BF16),
-            jax.ShapeDtypeStruct((64, 32, 128), BF16),
+            pltpu.VMEM((16, 32, 256), BF16),
+            pltpu.VMEM((32, 2, 32, 128), BF16),
         ),
         in_specs=[hbm] * 16,
-        out_specs=(hbm, hbm),
+        out_specs=(vmem, vmem),
         scratch_shapes=[
             buf(16, 32, 256), pltpu.VMEM((2, 512, 128), F32), buf(32, 16, 256), buf(2, 256, 256),
             line(256), line(256), line(256), line(256), line(256), line(256), line(128),
             buf(256, 256), buf(256, 256), buf(256, 256), buf(256, 256), buf(256, 256),
             buf(64, 256), buf(1024, 128), pltpu.VMEM((1024, 128), F32),
-            buf(768, 256), pltpu.VMEM((256, 128), F32), buf(8, 48, 256), pltpu.VMEM((256, 256), F32), buf(4096, 512),
-            buf(2, 256, 256), buf(32, 16, 256), buf(16, 32, 256), buf(2, 32, 256), buf(2, 32, 256),
+            buf(768, 256), pltpu.VMEM((256, 128), F32), buf(8, 48, 256), buf(8, 256, 256), pltpu.VMEM((256, 256), F32), buf(4096, 512),
+            buf(2, 256, 256), buf(32, 16, 256), buf(2, 32, 256), buf(2, 32, 256),
             buf(64, 32, 256), buf(32, 32, 256), pltpu.VMEM((2, 1024, 128), F32), buf(1024, 256), buf(16, 32, 4096),
-            buf(64, 32, 128),
             sem((16,)), sem((32,)), sem((32,)), sem((32,)), sem((32,)), sem((2,)), sem((2,)),
             sem((16,)), sem((16,)), sem((16,)), sem((16,)), sem((6,)), sem((6,)),
             sem((24,)), sem((24,)), sem((32,)), sem((32,)),
         ],
         compiler_params=pltpu.CompilerParams(
-            collective_id=0, has_side_effects=True, vmem_limit_bytes=60 * 2**20
+            collective_id=0, has_side_effects=True, vmem_limit_bytes=44 * 2**20
         ),
         name="evoformer",
     )(
+        *map(at_hbm, (
         alignment_embedding, row(heed_layer_gain), row(heed_layer_shift), probe_weights,
         lookup_weights, content_weights, sigmoid_weights, row(sigmoid_shift),
         final_weights, row(final_shift), row(tensor_layer_gain), row(tensor_layer_shift),
         first_factor_weights.T, second_factor_weights.T, couple_weights, row(couple_shift),
+        ))
     )
-    return upd, pair
+    return pl.pallas_call(
+        place,
+        out_shape=(
+            jax.ShapeDtypeStruct((16, 32, 256), BF16),
+            jax.ShapeDtypeStruct((64, 32, 128), BF16),
+        ),
+        in_specs=[vmem, vmem],
+        out_specs=(hbm, hbm),
+        scratch_shapes=[sem((2,))],
+        name="place",
+    )(at_vmem(upd), at_vmem(pair.reshape(64, 32, 128)))
 
 
 def solution(mesh):

time: 56.2 us -> 51.6 us (0.918)
  local copies, waits for them, and re-layouts: 2.52 us -> 0 us
  Pallas kernels: 52.8 us -> 50.9 us
    unnamed x4 -> x0, local copies, waits for them, and re-layouts: 2.52 us -> none
    pallas_call x1 -> x2, Pallas kernels: 52.8 us -> 50.9 us  [the longest x1 50 us: local(): pl.pallas_call(kernel, out_shape=(pltpu.VMEM((16, 32, 256), BF16), pltpu....]
where the time goes in v3:
time: 51.6 us; the launch traced here: 51.5 us
  Pallas kernels  50.9 us (99%)
  between operations  0.64 us (1%)
    pallas_call x1, Pallas kernels, local(): pl.pallas_call(kernel, out_shape=(pltpu.VMEM((16, 32, 256), BF16), pltpu....  50 us

profile of v3, /device:TPU:1, one launch (start us, length us, event | category | flops | bytes accessed | tf_op | source)
XLA Modules:
  0.0 51.5 jit_solution(13641600627105543701)
XLA Ops:
  0.6 50.0 %evoformer.1 = (bf16[16,32,256]{2,1,0:T(8,128)(2,1)S(1)}, bf16[32,2,32,128]{3,2,1,0:T(8,128)(2,1)S(1)}) custom-call(bf16[16,32,256]{2,1,0:T(8,128)(2,1)} %x_hbm.1, f32[1,256]{1,0:T(1,128)} %bitcast.13, f32[1,256]{1,0:T(1,128)} %bitcast.14, bf16[256,256]{1,0:T(8,128)(2,1)} %wq_hbm.1, bf16[256,256]{1,0:T(8,128)(2,1)} %wk_hbm.1, bf16[256,256]{1,0:T(8,128)(2,1)} %wv_hbm.1, ...), custom_call_target="tpu_custom_call" | custom-call | tf_op jit(solution)/shard_map/evoformer/pallas_call | solution.py:339
  50.6 0.9 %place.1 = (bf16[16,32,256]{2,1,0:T(8,128)(2,1)}, bf16[64,32,128]{2,1,0:T(8,128)(2,1)}) custom-call(bf16[16,32,256]{2,1,0:T(8,128)(2,1)S(1)} %get-tuple-element.4.upd, bf16[64,32,128]{2,1,0:T(8,128)(2,1)S(1)} %bitcast.10), custom_call_target="tpu_custom_call" | custom-call | tf_op jit(solution)/shard_map/place/pallas_call | solution.py:371

commit v4 on v3

--- a/solution.py
+++ b/solution.py
@@ -13,6 +13,7 @@
 F32 = jnp.float32
 MESH = pl.DeviceIdType.MESH
 SPREAD = (4, 5, 3, 6, 2, 7, 1)
+FARTHEST = (8, 7, 9, 6, 10, 5, 11, 4, 12, 3, 13, 2, 14, 1, 15)
 SCALE = 1.4426950408889634 / 32.0**0.5
 
 
@@ -90,18 +91,17 @@
     seq_dev = [((q + k) % 16, r) for k in range(16)]
     y_dev = [(((y + k) % 8) * 2 + zl, r) for k in range(8)]
     zl_dev = (y * 2 + 1 - zl, r)
+    barrier = pltpu.get_barrier_semaphore()
+    for k in FARTHEST:
+        pl.semaphore_signal(barrier, inc=1, device_id=seq_dev[k], device_id_type=MESH)
     zh_dev = [(q, res(x, (zh + k) % 4, c)) for k in range(4)]
     x_dev = [(q, res((x + k) % 4, zh, c)) for k in range(4)]
     core_dev = (q, res(x, zh, 1 - c))
     relay_x, relay_zh = relay_of(plane, y, zl)
     relay_dev = (plane, res(relay_x, relay_zh, c))
-    source = [[chunk_at(q, (x + 4 - i) % 4, (zh + 4 - j) % 4) for j in range(4)] for i in range(4)]
-    held = [[source[i][j][0] * 2 + source[i][j][1] for j in range(4)] for i in range(4)]
-    from_dev = (held[0][0], 2 * q + c)
-
-    barrier = pltpu.get_barrier_semaphore()
-    greet = seq_dev[1:] + zh_dev[1:] + x_dev[1:] + [core_dev, from_dev]
-    for dev in greet:
+    from_y, from_zl = chunk_at(q, x, zh)
+    others = zh_dev[1:] + x_dev[1:] + [core_dev, (from_y * 2 + from_zl, 2 * q + c)]
+    for dev in others:
         pl.semaphore_signal(barrier, inc=1, device_id=dev, device_id_type=MESH)
 
     loads = [
@@ -128,13 +128,16 @@
     for m in range(2):
         xg[m, mine, :] = xt[2 * q + m]
 
-    pl.semaphore_wait(barrier, len(greet))
-    order = (8, 7, 9, 6, 10, 5, 11, 4, 12, 3, 13, 2, 14, 1, 15)
+    pl.semaphore_wait(barrier, 15 + len(others))
+    order = FARTHEST
     turn = [
         [go(seq_dev[k], xt.at[2 * seq_dev[k][0] + m], xg.at[m, mine, :], a_send, a_recv, m * 16 + k)
          for k in order]
         for m in range(2)
     ]
+
+    source = [[chunk_at(q, (x + 4 - i) % 4, (zh + 4 - j) % 4) for j in range(4)] for i in range(4)]
+    held = [[source[i][j][0] * 2 + source[i][j][1] for j in range(4)] for i in range(4)]
 
     for copy in loads[1:]:
         copy.wait()
@@ -218,15 +221,23 @@
         go(core_dev, here, here, lc_send, lc_recv, m * 16 + j)
 
     z_left = []
-    for m in range(2):
+
+    def take(m):
         relay[m].wait_recv()
         here = slot(c, held[0][0], m)
         z_left.append({k: go(zh_dev[k], here, here, lz_send, lz_recv, m * 3 + k - 1) for k in (2, 1, 3)})
         pass_on(0, m)
+
+    def right_on(m):
         for k in SPREAD[::-1]:
             along[m][k].wait_recv()
             here = right.at[(((y + 8 - k) % 8) * 2 + zl) * 2 + m]
             across.append(go(zl_dev, here, here, rz_send, rz_recv, m * 8 + k))
+
+    take(0)
+    take(1)
+    right_on(0)
+    right_on(1)
     send_back(0)
     send_back(1)
     for m in range(2):

time: 51.6 us -> 51 us (0.988); the launches traced: 51.5 us -> 50.1 us
  Pallas kernels: 50.9 us -> 49.5 us
    pallas_call x1, Pallas kernels: 50 us -> 48.6 us  [local(): pl.pallas_call(kernel, out_shape=(pltpu.VMEM((16, 32, 256), BF16), pltpu....]
where the time goes in v4:
time: 51 us; the launch traced here: 50.1 us
  Pallas kernels  49.5 us (97%)
  between operations  0.64 us (1%)
    pallas_call x1, Pallas kernels, local(): pl.pallas_call(kernel, out_shape=(pltpu.VMEM((16, 32, 256), BF16), pltpu....  48.6 us

profile of v4, /device:TPU:1, one launch (start us, length us, event | category | flops | bytes accessed | tf_op | source)
XLA Modules:
  0.0 50.1 jit_solution(17487252055899356149)
XLA Ops:
  0.6 48.6 %evoformer.1 = (bf16[16,32,256]{2,1,0:T(8,128)(2,1)S(1)}, bf16[32,2,32,128]{3,2,1,0:T(8,128)(2,1)S(1)}) custom-call(bf16[16,32,256]{2,1,0:T(8,128)(2,1)} %x_hbm.1, f32[1,256]{1,0:T(1,128)} %bitcast.13, f32[1,256]{1,0:T(1,128)} %bitcast.14, bf16[256,256]{1,0:T(8,128)(2,1)} %wq_hbm.1, bf16[256,256]{1,0:T(8,128)(2,1)} %wk_hbm.1, bf16[256,256]{1,0:T(8,128)(2,1)} %wv_hbm.1, ...), custom_call_target="tpu_custom_call" | custom-call | tf_op jit(solution)/shard_map/evoformer/pallas_call | solution.py:350
  49.2 0.9 %place.1 = (bf16[16,32,256]{2,1,0:T(8,128)(2,1)}, bf16[64,32,128]{2,1,0:T(8,128)(2,1)}) custom-call(bf16[16,32,256]{2,1,0:T(8,128)(2,1)S(1)} %get-tuple-element.4.upd, bf16[64,32,128]{2,1,0:T(8,128)(2,1)S(1)} %bitcast.10), custom_call_target="tpu_custom_call" | custom-call | tf_op jit(solution)/shard_map/place/pallas_call | solution.py:382

commit v5 on v4

--- a/solution.py
+++ b/solution.py
@@ -238,12 +238,12 @@
     take(1)
     right_on(0)
     right_on(1)
-    send_back(0)
-    send_back(1)
     for m in range(2):
         for k in (1, 3, 2):
             z_left[m][k].wait_recv()
             pass_on(k, m)
+    send_back(0)
+    send_back(1)
 
     def outer_of(c_, m, pick):
         at = [(c_ * 16 + held[i][j]) * 2 + m for i, j in pick]

time: 51 us -> 51.6 us (1.012)
  the two profiles are of different devices: /device:TPU:1 before, /device:TPU:58 now
where the time goes in v5:
time: 51.6 us; the launch traced here: 51.5 us
  Pallas kernels  50.9 us (99%)
  between operations  0.64 us (1%)
    pallas_call x1, Pallas kernels, local(): pl.pallas_call(kernel, out_shape=(pltpu.VMEM((16, 32, 256), BF16), pltpu....  50 us

profile of v5, /device:TPU:58, one launch (start us, length us, event | category | flops | bytes accessed | tf_op | source)
XLA Modules:
  0.0 51.5 jit_solution(13810886572303338856)
XLA Ops:
  0.6 50.0 %evoformer.1 = (bf16[16,32,256]{2,1,0:T(8,128)(2,1)S(1)}, bf16[32,2,32,128]{3,2,1,0:T(8,128)(2,1)S(1)}) custom-call(bf16[16,32,256]{2,1,0:T(8,128)(2,1)} %x_hbm.1, f32[1,256]{1,0:T(1,128)} %bitcast.13, f32[1,256]{1,0:T(1,128)} %bitcast.14, bf16[256,256]{1,0:T(8,128)(2,1)} %wq_hbm.1, bf16[256,256]{1,0:T(8,128)(2,1)} %wk_hbm.1, bf16[256,256]{1,0:T(8,128)(2,1)} %wv_hbm.1, ...), custom_call_target="tpu_custom_call" | custom-call | tf_op jit(solution)/shard_map/evoformer/pallas_call | solution.py:350
  50.6 0.9 %place.1 = (bf16[16,32,256]{2,1,0:T(8,128)(2,1)}, bf16[64,32,128]{2,1,0:T(8,128)(2,1)}) custom-call(bf16[16,32,256]{2,1,0:T(8,128)(2,1)S(1)} %get-tuple-element.4.upd, bf16[64,32,128]{2,1,0:T(8,128)(2,1)S(1)} %bitcast.10), custom_call_target="tpu_custom_call" | custom-call | tf_op jit(solution)/shard_map/place/pallas_call | solution.py:382
